TPU v7x, 256 devices: a whole 4x4x8 slice. The times are simulated.
256 devices in a mesh: chan: 64 (over y_hi, x, z), win: 4 (over y_lo, core).
Axes of the slice: x: 4, y: 4 (y_hi: 2, y_lo: 2; y = y_hi * 2 + y_lo), z: 8, core: 2. Of those that a mesh axis runs over, the one named last changes fastest.
Arguments:
- spectra: bfloat16 [64, 128, 128, 2, 128], P('chan', None, 'win'), may hold values from -6 to 6
- counts: int32 [128, 64], P('win'), may hold values from 1 to 256
- partner: int32 [2, 64], replicated, may hold values from 0 to 63, as said below
Outputs:
- cross: bfloat16 [64, 2, 128, 128, 256], P('win', None, 'chan')
Inputs may be any that keep to these rules, and one draw needn't show every extreme that they name: Each row of partner is one cycle through all 64 blocks: a permutation with no block its own partner and no two blocks each other's partners.
All inputs are finite; a program needn't handle non-finite values.
Results may differ from a plain program's by a relative error of at most 0.015.
Values may be sent and summed in bfloat16 or wider, within the bound.
No kernel may reach another device: no remote copies, remote signals or barrier semaphores. Data moves between devices by JAX's collectives and lax.ppermute only.
A program may use at most 128 MiB of HBM per device.

v0:
```python
import jax
import jax.numpy as jnp
from jax import lax
from jax.sharding import PartitionSpec as P

W_DEV = 32
NSAMP = 256
EPS = 1e-06


def stack_blocks(blocks, scale, mate_index, first, count):
    own = lax.dynamic_slice_in_dim(blocks, first, count, 0)
    mates = jnp.take(blocks, mate_index, axis=0)
    weighted = (scale[:, :, None, :, :, None, None] * own[:, None]).astype(jnp.bfloat16)
    rotated = jnp.stack([-mates[..., 1, :], mates[..., 0, :]], axis=-2)
    paired = jnp.stack([mates, rotated], axis=-2)
    return jnp.einsum(
        "nrfgwkc,nrfgwkod->nrfgcod", weighted, paired, preferred_element_type=jnp.float32
    )


def weights_of(tallies, partner):
    columns = tallies.astype(jnp.float32).T
    return jnp.minimum(columns[None], jnp.take(columns, partner, axis=0)) / NSAMP


def per_device(spectra, counts, partner):
    values = spectra.astype(jnp.float32)
    power = jnp.mean(jnp.sum(values * values, axis=3), axis=1)
    whitened = (values * lax.rsqrt(power + EPS)[:, None, :, None, :]).astype(jnp.bfloat16)
    mixed = lax.all_to_all(whitened, "chan", split_axis=1, concat_axis=0, tiled=True)
    nblocks = partner.shape[1]
    width = mixed.shape[4]
    local_bins = mixed.shape[1]
    rounds = partner.shape[0]
    groups = lax.axis_size("win")
    chosen = nblocks // groups
    first = lax.axis_index("win") * chosen
    gathered = lax.all_gather(mixed, "win", axis=2, tiled=True)
    tallies = lax.all_gather(counts, "win", axis=0, tiled=True)
    weight = weights_of(tallies, partner)
    norm = jnp.sqrt(jnp.sum(weight * weight, axis=2))
    blocks = gathered.reshape(nblocks, local_bins, groups, W_DEV, 2, width)
    own_scales = jnp.transpose(lax.dynamic_slice_in_dim(weight, first, chosen, 1), (1, 0, 2))
    scale = own_scales.reshape(chosen, rounds, groups, W_DEV)
    mate_index = jnp.transpose(lax.dynamic_slice_in_dim(partner, first, chosen, 1))
    partial_value = stack_blocks(blocks, scale, mate_index, first, chosen)
    partial_value = lax.optimization_barrier(partial_value.astype(jnp.bfloat16))
    total = jnp.sum(partial_value.astype(jnp.float32), axis=3)
    norm_rows = jnp.transpose(lax.dynamic_slice_in_dim(norm, first, chosen, 1))
    shaped = total.reshape(chosen, rounds, local_bins, width, 2 * width)
    result = shaped / norm_rows[:, :, None, None, None]
    return result.astype(jnp.bfloat16)


def solution(mesh):
    placed = (P("chan", None, "win", None, None), P("win", None), P())
    return jax.shard_map(
        per_device,
        mesh=mesh,
        in_specs=placed,
        out_specs=P("win", None, "chan", None, None),
        check_vma=False,
    )
```

profile of v0, /device:TPU:1, one launch (start us, length us, event | category | flops | bytes accessed | tf_op | source)
XLA Modules:
  0.0 240.4 jit_solution(3108517690756288380)
XLA Ops:
  6.5 0.0 all-gather.2.cloned.1.call-start
  6.5 3.8 %fusion.4 = f32[32,128]{1,0:T(8,128)S(1)} fusion(bf16[1,128,32,2,128]{4,3,2,1,0:T(2,128)(2,1)} %param.3), kind=kLoop, calls=%fused_computation.12 | loop fusion | flops 3141632 | bytes 2113536 | tf_op jit(solution)/shard_map/reduce_sum | solution.py:29
  10.4 3.8 %fusion.5 = bf16[1,128,32,2,128]{4,3,2,0,1:T(2,128)(2,1)S(1)} fusion(bf16[1,128,32,2,128]{4,3,2,1,0:T(2,128)(2,1)} %param.3, f32[32,128]{1,0:T(8,128)S(1)} %add_rsqrt_fusion), kind=kLoop, calls=%fused_computation.13 | loop fusion | flops 3145728 | bytes 4210688 | tf_op jit(solution)/shard_map/convert_element_type | solution.py:30
  14.2 63.5 %all_to_all.12 = bf16[1,128,32,2,128]{4,3,2,0,1:T(2,128)(2,1)S(1)} all-to-all(bf16[1,128,32,2,128]{4,3,2,0,1:T(2,128)(2,1)S(1)} %fusion.5), channel_id=1, replica_groups=mesh['chan'=64,'win'=4] {'chan'}, dimensions={1} | all-to-all | bytes 4194304 | tf_op jit(solution)/shard_map/all_to_all | solution.py:31
  77.7 0.0 copy-start.2
  77.7 0.0 copy-start.1
  77.7 1.9 copy.36
  79.6 0.0 all-gather.2.cloned.1.call-update
  79.6 0.0 copy-done.2
  79.6 0.1 compare_and_fusion
  79.7 0.1 copy.39
  79.8 0.1 reshape.56
  79.9 0.1 copy.38
  80.0 0.0 copy-done.1
  80.0 9.0 %all_gather.6 = s32[128,64]{1,0:T(8,128)S(1)} all-gather(s32[32,64]{1,0:T(8,128)S(1)} %copy-done.1), channel_id=1, replica_groups=mesh['chan'=64,'win'=4] {'win'}, dimensions={0}, use_global_device_ids=true | all-gather | bytes 40960 | tf_op jit(solution)/shard_map/all_gather | solution.py:40
  89.0 0.1 copy.33
  89.1 0.1 reshape.48
  89.2 0.6 gather_fusion
  89.9 0.2 multiply_reduce_fusion
  90.1 0.1 mul.33
  90.2 0.1 dynamic-slice_bitcast_fusion.1
  90.3 0.1 copy.43
  90.3 72.9 %all-gather.2.cloned.1.call-done = bf16[64,2,128,2,128]{4,2,3,1,0:T(8,128)(2,1)} async-done(((bf16[64,2,32,2,128]{4,2,3,1,0:T(8,128)(2,1)}), bf16[64,2,128,2,128]{4,2,3,1,0:T(8,128)(2,1)}) %all-gather.2.cloned.1.call-update) | async-done | bytes 8388624 | tf_op jit(solution)/shard_map/all_gather | solution.py:39
  163.2 9.2 %copy.40 = bf16[64,2,4,32,2,128]{5,3,4,2,1,0:T(8,128)(2,1)} copy(bf16[64,2,4,32,2,128]{5,3,2,4,1,0:T(8,128)(2,1)} %bitcast.35) | data formatting | bytes 16777216 | tf_op jit(solution)/shard_map/reshape | solution.py:43
  172.4 6.5 %gather_fusion.1 = bf16[32,2,4,32,2,128]{5,3,4,2,1,0:T(8,128)(2,1)} fusion(bf16[64,2,4,32,2,128]{5,3,4,2,1,0:T(8,128)(2,1)} %copy.40, s32[1024]{0:T(1024)S(1)} %pad_clamp_fusion), kind=kCustom, calls=%fused_computation.1 | custom fusion | bytes 8388736 | tf_op jit(solution)/shard_map/jit(_take)/gather | solution.py:13
  178.8 2.6 %broadcast_select_fusion = bf16[16,2,2,4,32,2,128]{6,4,5,3,2,1,0:T(8,128)(2,1)S(1)} fusion(bf16[16,2,2,4,32,2,128]{6,4,5,3,2,1,0:T(8,128)(2,1)} %bitcast.33, pred[16,2]{1,0:T(8,128)(4,1)S(1)} %copy.38), kind=kLoop, calls=%fused_computation.18 | loop fusion | flops 2097152 | bytes 8388640 | tf_op jit(solution)/shard_map/jit(_take)/select_n | solution.py:13
  181.5 0.0 copy-start
  181.5 0.4 slice_negate_fusion
  181.9 1.8 copy-done
  183.7 0.5 broadcast_select_fusion.1
  184.2 2.4 maximum_bitcast_fusion
  186.5 11.9 %bitcast_convert_fusion = bf16[16,2,2,4,128,2,128]{6,4,5,3,2,1,0:T(8,128)(2,1)} fusion(bf16[16,2,2,4,32,2,1,128]{7,4,5,6,3,2,1,0:T(8,128)(2,1)} %maximum_bitcast_fusion, bf16[16,2,2,4,32,2,1,128]{7,4,5,6,3,2,1,0:T(8,128)(2,1)S(1)} %broadcast_select_fusion.1, f32[16,2,4,32]{3,2,0,1:T(4,128)S(1)} %mul.33, bf16[64,2,4,32,2,128]{5,3,2,4,1,0:T(8,128)(2,1)} %bitcast.36, ...), kind=kOutput, calls=%fused_computation.2 | convolution fusion | flops 1104150528 | bytes 27279364 | tf_op jit(solution)/shard_map/nrfgwkc,nrfgwkod->nrfgcod/dot_general | solution.py:17
  198.4 13.0 %convert_reduce_fusion = f32[16,2,2,128,2,128]{5,3,4,2,1,0:T(8,128)} fusion(bf16[16,2,2,4,128,2,128]{6,4,5,3,2,1,0:T(8,128)(2,1)} %bitcast_convert_fusion), kind=kLoop, calls=%fused_computation.3 | loop fusion | flops 14680064 | bytes 25165824 | tf_op jit(solution)/shard_map/reduce_sum | solution.py:49
  211.4 9.3 %copy.42 = f32[16,2,2,128,2,128]{3,5,4,2,1,0:T(8,128)} copy(f32[16,2,2,128,2,128]{5,3,4,2,1,0:T(8,128)} %convert_reduce_fusion) | data formatting | bytes 16777216 | tf_op jit(solution)/shard_map/reduce_sum | solution.py:49
  220.7 6.5 %fusion.3 = bf16[16,2,2,128,256]{3,4,2,1,0:T(8,128)(2,1)} fusion(f32[16,2,2,128,2,128]{3,5,4,2,1,0:T(8,128)} %copy.42, f32[16,2]{1,0:T(8,128)S(1)} %copy.43), kind=kLoop, calls=%fused_computation.8 | loop fusion | flops 4194304 | bytes 12583040 | tf_op jit(solution)/shard_map/convert_element_type | solution.py:53
  227.2 6.4 %copy.44 = bf16[16,2,2,128,256]{4,3,2,1,0:T(8,128)(2,1)} copy(bf16[16,2,2,128,256]{3,4,2,1,0:T(8,128)(2,1)} %fusion.3) | data formatting | bytes 8388608 | tf_op jit(solution)/shard_map/convert_element_type | solution.py:53
  (8 shorter events, 0.1 us)
Async XLA Ops:
  6.5 156.7 %all-gather.2.cloned.1.call-start = ((), (), s32[]{:S(2)}) async-start(), calls=%async_computation.1 | async-start | bytes 10485760 | tf_op jit(solution)/shard_map/all_gather | solution.py:39
  77.7 1.9 copy-start.2
  77.7 2.3 copy-start.1
  181.5 2.2 copy-start
Sparse Core Ops, SparseCore 0:
  79.7 83.4 all-gather.1
where the time goes:
time: 241 us; the launch traced here: 240 us
  waiting for transfers between devices  72.9 us (30%)
  blocking collectives  72.6 us (30%)
  local copies, waits for them, and re-layouts  36.3 us (15%)
  other arithmetic  33.3 us (14%)
  between operations  13.5 us (6%)
  matrix products  11.9 us (5%)
    all_gather x1, waiting for transfers between devices, per_device(): gathered = lax.all_gather(mixed, 'win', axis=2, tiled=True)  72.9 us
    all_to_all x1, blocking collectives, per_device(): lax.all_to_all(whitened, 'chan', split_axis=1, concat_axis=0, tiled=True)  63.5 us
    reduce_sum x1, other arithmetic, per_device(): total = jnp.sum(partial_value.astype(jnp.float32), axis=3)  13 us
    dot_general x1, matrix products, stack_blocks(): jnp.einsum('nrfgwkc,nrfgwkod->nrfgcod', weighted, paired, preferred_eleme...  11.9 us
    reduce_sum x1, local copies, waits for them, and re-layouts, per_device(): total = jnp.sum(partial_value.astype(jnp.float32), axis=3)  9.27 us
    reshape x1, local copies, waits for them, and re-layouts, per_device(): blocks = gathered.reshape(nblocks, local_bins, groups, W_DEV, 2, width)  9.15 us
    all_gather x1, blocking collectives, per_device(): tallies = lax.all_gather(counts, 'win', axis=0, tiled=True)  9.03 us
    convert_element_type x1, other arithmetic, per_device(): return result.astype(jnp.bfloat16)  6.5 us
  transfers between devices with their start and end apart: 1, of which 1 were waited for; matrix products, arithmetic and copies ran while one was open for 1% of the time, Pallas kernels for 0%

commit v1 on v0

--- a/solution.py
+++ b/solution.py
@@ -36,7 +36,9 @@
     groups = lax.axis_size("win")
     chosen = nblocks // groups
     first = lax.axis_index("win") * chosen
-    gathered = lax.all_gather(mixed, "win", axis=2, tiled=True)
+    gathered = jnp.concatenate(
+        lax.all_to_all(jnp.stack([mixed] * lax.axis_size("win")), "win", 0, 0), axis=2
+    )
     tallies = lax.all_gather(counts, "win", axis=0, tiled=True)
     weight = weights_of(tallies, partner)
     norm = jnp.sqrt(jnp.sum(weight * weight, axis=2))

time: 241 us -> 244 us (1.012)
  blocking collectives: 72.6 us -> 157 us
  waiting for transfers between devices: 72.9 us -> 0.01 us
  between operations: 13.5 us -> 0.11 us
  starting transfers between devices: 0.01 us -> 9.53 us
  local copies, waits for them, and re-layouts: 36.3 us -> 32.9 us
    all_gather x1, blocking collectives: 9.03 us -> 93.8 us  [per_device(): tallies = lax.all_gather(counts, 'win', axis=0, tiled=True)]
    all_gather x1 -> x0, waiting for transfers between devices: 72.9 us -> none  [per_device(): gathered = lax.all_gather(mixed, 'win', axis=2, tiled=True)]
    all_to_all x0 -> x1, starting transfers between devices: none -> 9.53 us  [per_device(): lax.all_to_all(jnp.stack([mixed] * lax.axis_size('win')), 'win', 0, 0)]
    reshape x1 -> x0, local copies, waits for them, and re-layouts: 9.15 us -> none  [per_device(): blocks = gathered.reshape(nblocks, local_bins, groups, W_DEV, 2, width)]
    another operation x0 -> x2, local copies, waits for them, and re-layouts: none -> 6.23 us  [per_device(): jnp.stack([mixed] * lax.axis_size('win'))]
    gather x1 -> x2, local copies, waits for them, and re-layouts: 6.48 us -> 9.67 us  [stack_blocks(): mates = jnp.take(blocks, mate_index, axis=0)]
  transfers between devices with their start and end apart: 1 -> 1, of which waited for: 1 -> 0; matrix products, arithmetic and copies ran while one was open for 1% -> 1% of each run, Pallas kernels for 0% -> 0%
where the time goes in v1:
time: 244 us; the launch traced here: 243 us
  blocking collectives  157 us (64%)
  local copies, waits for them, and re-layouts  32.9 us (13%)
  other arithmetic  31.2 us (13%)
  matrix products  11.9 us (5%)
  starting transfers between devices  9.53 us (4%)
    all_gather x1, blocking collectives, per_device(): tallies = lax.all_gather(counts, 'win', axis=0, tiled=True)  93.8 us
    all_to_all x1, blocking collectives, per_device(): lax.all_to_all(whitened, 'chan', split_axis=1, concat_axis=0, tiled=True)  63.5 us
    reduce_sum x1, other arithmetic, per_device(): total = jnp.sum(partial_value.astype(jnp.float32), axis=3)  13 us
    dot_general x1, matrix products, stack_blocks(): jnp.einsum('nrfgwkc,nrfgwkod->nrfgcod', weighted, paired, preferred_eleme...  11.9 us
    gather x2, local copies, waits for them, and re-layouts, stack_blocks(): mates = jnp.take(blocks, mate_index, axis=0)  9.67 us
    all_to_all x1, starting transfers between devices, per_device(): lax.all_to_all(jnp.stack([mixed] * lax.axis_size('win')), 'win', 0, 0)  9.53 us
    reduce_sum x1, local copies, waits for them, and re-layouts, per_device(): total = jnp.sum(partial_value.astype(jnp.float32), axis=3)  9.27 us
    convert_element_type x1, other arithmetic, per_device(): return result.astype(jnp.bfloat16)  6.5 us
  transfers between devices with their start and end apart: 1, of which 0 were waited for; matrix products, arithmetic and copies ran while one was open for 1% of the time, Pallas kernels for 0%

profile of v1, /device:TPU:1, one launch (start us, length us, event | category | flops | bytes accessed | tf_op | source)
XLA Modules:
  0.0 242.9 jit_solution(15499896368749880166)
XLA Ops:
  0.0 3.8 %fusion.4 = f32[32,128]{1,0:T(8,128)S(1)} fusion(bf16[1,128,32,2,128]{4,3,2,1,0:T(2,128)(2,1)} %param.3), kind=kLoop, calls=%fused_computation.12 | loop fusion | flops 3141632 | bytes 2113536 | tf_op jit(solution)/shard_map/reduce_sum | solution.py:29
  3.8 3.8 %fusion.5 = bf16[1,128,32,2,128]{4,3,2,0,1:T(2,128)(2,1)S(1)} fusion(bf16[1,128,32,2,128]{4,3,2,1,0:T(2,128)(2,1)} %param.3, f32[32,128]{1,0:T(8,128)S(1)} %add_rsqrt_fusion), kind=kLoop, calls=%fused_computation.13 | loop fusion | flops 3145728 | bytes 4210688 | tf_op jit(solution)/shard_map/convert_element_type | solution.py:30
  7.6 63.5 %all_to_all.14 = bf16[1,128,32,2,128]{4,3,2,0,1:T(2,128)(2,1)S(1)} all-to-all(bf16[1,128,32,2,128]{4,3,2,0,1:T(2,128)(2,1)S(1)} %fusion.5), channel_id=1, replica_groups=mesh['chan'=64,'win'=4] {'chan'}, dimensions={1} | all-to-all | bytes 4194304 | tf_op jit(solution)/shard_map/all_to_all | solution.py:31
  71.2 0.6 copy.30
  71.8 5.6 %stack.21 = bf16[4,64,2,32,2,128]{5,3,4,2,1,0:T(8,128)(2,1)} broadcast(bf16[64,2,32,2,128]{4,2,3,1,0:T(8,128)(2,1)S(1)} %copy.30), dimensions={1,2,3,4,5} | broadcast | bytes 10485760 | tf_op jit(solution)/shard_map/stack | solution.py:40
  77.4 0.0 copy-start.1
  77.4 0.0 copy-start
  77.4 9.5 %all-to-all-start.1 = ((bf16[4,64,2,32,2,128]{5,3,4,2,1,0:T(8,128)(2,1)}), bf16[4,64,2,32,2,128]{5,3,4,2,1,0:T(8,128)(2,1)}, u32[]{:S(2)}, u32[]{:S(2)}) async-start(bf16[4,64,2,32,2,128]{5,3,4,2,1,0:T(8,128)(2,1)} %stack.21), calls=%async_computation.1 | async-start | bytes 16777216 | tf_op jit(solution)/shard_map/all_to_all | solution.py:40
  86.9 0.0 copy-done.1
  86.9 0.1 compare_and_fusion
  87.0 0.1 copy.33
  87.1 0.1 reshape.58
  87.2 0.1 copy.32
  87.3 0.0 copy-done
  87.3 93.8 %all_gather.3 = s32[128,64]{1,0:T(8,128)S(1)} all-gather(s32[32,64]{1,0:T(8,128)S(1)} %copy-done), channel_id=1, replica_groups=mesh['chan'=64,'win'=4] {'win'}, dimensions={0}, use_global_device_ids=true | all-gather | bytes 40960 | tf_op jit(solution)/shard_map/all_gather | solution.py:42
  181.1 0.1 copy.27
  181.2 0.1 reshape.50
  181.3 0.6 gather_fusion
  181.9 0.2 multiply_reduce_fusion
  182.1 0.1 mul.33
  182.2 0.1 dynamic-slice_bitcast_fusion.1
  182.3 0.1 copy.38
  182.4 0.0 all-to-all-done.1
  182.4 6.5 %gather_fusion.1 = bf16[32,2,4,32,2,128]{5,3,4,1,2,0:T(8,128)(2,1)} fusion(bf16[64,2,4,32,2,128]{5,3,4,1,0,2:T(8,128)(2,1)} %bitcast.9, s32[1024]{0:T(1024)S(1)} %pad_clamp_fusion), kind=kCustom, calls=%fused_computation.1 | custom fusion | bytes 8388736 | tf_op jit(solution)/shard_map/jit(_take)/gather | solution.py:13
  188.9 3.2 %copy.34 = bf16[32,2,4,32,2,128]{5,3,4,2,1,0:T(8,128)(2,1)S(1)} copy(bf16[32,2,4,32,2,128]{5,3,4,1,2,0:T(8,128)(2,1)} %gather_fusion.1) | data formatting | bytes 8388608 | tf_op jit(solution)/shard_map/jit(_take)/gather | solution.py:13
  192.1 0.5 broadcast_select_fusion
  192.6 0.4 slice_negate_fusion
  193.0 0.5 broadcast_select_fusion.1
  193.4 2.4 maximum_bitcast_fusion
  195.8 11.9 %bitcast_convert_fusion = bf16[16,2,2,4,128,2,128]{6,4,5,3,2,1,0:T(8,128)(2,1)} fusion(bf16[16,2,2,4,32,2,1,128]{7,4,5,6,3,2,1,0:T(8,128)(2,1)} %maximum_bitcast_fusion, bf16[16,2,2,4,32,2,1,128]{7,4,5,6,3,2,1,0:T(8,128)(2,1)S(1)} %broadcast_select_fusion.1, f32[16,2,4,32]{3,2,0,1:T(4,128)S(1)} %mul.33, bf16[4,64,2,32,2,128]{5,3,4,2,1,0:T(8,128)(2,1)} %all-to-all-done.1, ...), kind=kOutput, calls=%fused_computation.2 | convolution fusion | flops 1104150528 | bytes 27279364 | tf_op jit(solution)/shard_map/nrfgwkc,nrfgwkod->nrfgcod/dot_general | solution.py:17
  207.7 13.0 %convert_reduce_fusion = f32[16,2,2,128,2,128]{5,3,4,2,1,0:T(8,128)} fusion(bf16[16,2,2,4,128,2,128]{6,4,5,3,2,1,0:T(8,128)(2,1)} %bitcast_convert_fusion), kind=kLoop, calls=%fused_computation.3 | loop fusion | flops 14680064 | bytes 25165824 | tf_op jit(solution)/shard_map/reduce_sum | solution.py:51
  220.7 9.3 %copy.37 = f32[16,2,2,128,2,128]{3,5,4,2,1,0:T(8,128)} copy(f32[16,2,2,128,2,128]{5,3,4,2,1,0:T(8,128)} %convert_reduce_fusion) | data formatting | bytes 16777216 | tf_op jit(solution)/shard_map/reduce_sum | solution.py:51
  230.0 6.5 %fusion.3 = bf16[16,2,2,128,256]{3,4,2,1,0:T(8,128)(2,1)} fusion(f32[16,2,2,128,2,128]{3,5,4,2,1,0:T(8,128)} %copy.37, f32[16,2]{1,0:T(8,128)S(1)} %copy.38), kind=kLoop, calls=%fused_computation.8 | loop fusion | flops 4194304 | bytes 12583040 | tf_op jit(solution)/shard_map/convert_element_type | solution.py:55
  236.5 6.4 %copy.39 = bf16[16,2,2,128,256]{4,3,2,1,0:T(8,128)(2,1)} copy(bf16[16,2,2,128,256]{3,4,2,1,0:T(8,128)(2,1)} %fusion.3) | data formatting | bytes 8388608 | tf_op jit(solution)/shard_map/convert_element_type | solution.py:55
  (8 shorter events, 0.1 us)
Async XLA Ops:
  77.4 9.5 %copy-start.1 = (s32[2,64]{1,0:T(2,128)S(1)}, s32[2,64]{1,0:T(2,128)}, u32[]{:S(2)}) copy-start(s32[2,64]{1,0:T(2,128)} %param.5) | copy-start | bytes 1540
  77.4 9.9 %copy-start = (s32[32,64]{1,0:T(8,128)S(1)}, s32[32,64]{1,0:T(8,128)}, u32[]{:S(2)}) copy-start(s32[32,64]{1,0:T(8,128)} %param.4) | copy-start | bytes 24580
  77.4 105.0 %all-to-all-start.1 = ((bf16[4,64,2,32,2,128]{5,3,4,2,1,0:T(8,128)(2,1)}), bf16[4,64,2,32,2,128]{5,3,4,2,1,0:T(8,128)(2,1)}, u32[]{:S(2)}, u32[]{:S(2)}) async-start(bf16[4,64,2,32,2,128]{5,3,4,2,1,0:T(8,128)(2,1)} %stack.21), calls=%async_computation.1 | async-start | bytes 16777216 | tf_op jit(solution)/shard_map/all_to_all | solution.py:40
